TPU v7x, 128 devices: a whole 4x4x4 slice. The times are simulated.
128 devices in a mesh: row: 8 (over z_hi, x), col: 16 (over y, z_lo, core).
Axes of the slice: x: 4, y: 4, z: 4 (z_hi: 2, z_lo: 2; z = z_hi * 2 + z_lo), core: 2. Of those that a mesh axis runs over, the one named last changes fastest.
Arguments:
- pair_repr: bfloat16 [1024, 1024, 128], P('row', 'col'), may hold values from -6 to 6
- logit_cotangent: bfloat16 [1024, 1024, 128], P('row', 'col'), may hold values from -6 to 6
- pair_mask: int32 [1024, 1024], P('row', 'col'), may hold values 0 or 1
- single_repr: bfloat16 [1024, 384], P(('row', 'col')), may hold values from -6 to 6
- token_index: int32 [1024], replicated, may hold values from 0 to 2046, as said below
- pair_up: bfloat16 [128, 512], replicated, may hold values from -0.5 to 0.5
- pair_gate: bfloat16 [128, 512], replicated, may hold values from -0.5 to 0.5
- pair_down: bfloat16 [512, 128], replicated, may hold values from -0.25 to 0.25
- head_weight: bfloat16 [128, 128], replicated, may hold values from -0.5 to 0.5
- rel_table: bfloat16 [65, 128], replicated, may hold values from -3 to 3
- proj_row: bfloat16 [384, 128], replicated, may hold values from -0.3125 to 0.3125
- proj_col: bfloat16 [384, 128], replicated, may hold values from -0.3125 to 0.3125
- single_gate: bfloat16 [384, 1536], replicated, may hold values from -0.3125 to 0.3125
- single_up: bfloat16 [384, 1536], replicated, may hold values from -0.3125 to 0.3125
- single_down: bfloat16 [1536, 384], replicated, may hold values from -0.15625 to 0.15625
Outputs:
- pair_grad: bfloat16 [1024, 1024, 128], P('row', 'col')
- single_grad: bfloat16 [1024, 384], P(('row', 'col'))
- grad_pair_up: float32 [128, 512], replicated
- grad_pair_gate: float32 [128, 512], replicated
- grad_pair_down: float32 [512, 128], replicated
- grad_head: float32 [128, 128], replicated
- grad_rel: float32 [65, 128], replicated
- grad_proj_row: float32 [384, 128], replicated
- grad_proj_col: float32 [384, 128], replicated
- grad_single_gate: float32 [384, 1536], P(None, ('row', 'col'))
- grad_single_up: float32 [384, 1536], P(None, ('row', 'col'))
- grad_single_down: float32 [1536, 384], P(('row', 'col'))
Inputs may be any that keep to these rules, and one draw needn't show every extreme that they name: `token_index`: strictly increasing, entry 0 is 0, successive entries differ by 1 to 3, the last entry is 2046.
All inputs are finite; a program needn't handle non-finite values. No bound on the sum of `pair_mask` on one device may be relied on, other than what follows from the above.
Results may differ from a plain program's by a relative error of at most 0.018.
Values may be sent and summed in bfloat16 or wider, within the bound.
A program may use at most 128 MiB of HBM per device.

v0:
```python
import jax
import jax.numpy as jnp
from jax import lax
from jax.sharding import PartitionSpec as P

norm_eps = 1e-05


def gated_parts(gate):
    sigma = jax.nn.sigmoid(gate)
    return (gate * sigma, sigma * (1.0 + gate * (1.0 - sigma)))


def product(matrix_a, matrix_b):
    return jnp.dot(matrix_a, matrix_b, preferred_element_type=jnp.float32)


def product_left(matrix_a, matrix_b):
    return lax.dot_general(
        matrix_a, matrix_b, (((0,), (0,)), ((), ())), preferred_element_type=jnp.float32
    )


def product_right(matrix_a, matrix_b):
    return lax.dot_general(
        matrix_a, matrix_b, (((1,), (1,)), ((), ())), preferred_element_type=jnp.float32
    )


def single_forward(single_repr, single_gate, single_up, single_down):
    source = single_repr.astype(jnp.float32)
    inverse_rms = lax.rsqrt(jnp.mean(source * source, axis=-1, keepdims=True) + norm_eps)
    normed = source * inverse_rms
    normed_bf = normed.astype(jnp.bfloat16)
    gate_pre = product(normed_bf, single_gate)
    up_pre = product(normed_bf, single_up)
    silu_value, silu_slope = gated_parts(gate_pre)
    hidden = (silu_value * up_pre).astype(jnp.bfloat16)
    updated = (source + product(hidden, single_down)).astype(jnp.bfloat16)
    return (normed, inverse_rms, normed_bf, up_pre, silu_value, silu_slope, hidden, updated)


def single_backward(grad_in, saved_state, single_gate, single_up, single_down):
    normed, inverse_rms, normed_bf, up_pre, silu_value, silu_slope, hidden, updated = saved_state
    grad_bf = grad_in.astype(jnp.bfloat16)
    grad_hidden = product_right(grad_bf, single_down)
    grad_up = (grad_hidden * silu_value).astype(jnp.bfloat16)
    grad_gate = (grad_hidden * up_pre * silu_slope).astype(jnp.bfloat16)
    grad_normed = product_right(grad_gate, single_gate) + product_right(grad_up, single_up)
    grad_source = grad_in + inverse_rms * (
        grad_normed - normed * jnp.mean(grad_normed * normed, axis=-1, keepdims=True)
    )
    return (grad_source, grad_bf, grad_gate, grad_up)


def local_weight_sums(normed_bf, grad_bf, grad_gate, grad_up, hidden):
    return jnp.stack(
        [
            product_left(normed_bf, grad_gate),
            product_left(normed_bf, grad_up),
            product_left(grad_bf, hidden),
        ],
        axis=0,
    )


def pair_block(
    pair_blk,
    cot_blk,
    mirror_blk,
    row_blk,
    col_blk,
    row_pos,
    col_pos,
    rel_table,
    up_gate,
    pair_down,
    head_weight,
):
    n_rows, n_cols, pair_width = pair_blk.shape
    bin_count = mirror_blk.shape[2]
    rel_count = rel_table.shape[0]
    rel_span = (rel_count - 1) // 2
    pair_count = n_rows * n_cols
    offset = jnp.clip(row_pos[:, None] - col_pos[None, :], -rel_span, rel_span) + rel_span
    one_hot = offset.reshape(pair_count, 1) == jnp.arange(rel_count, dtype=jnp.int32)[None, :]
    hot_table = one_hot.astype(jnp.bfloat16)
    pair_in = (
        pair_blk.astype(jnp.float32)
        + row_blk.astype(jnp.float32)[:, None, :]
        + col_blk.astype(jnp.float32)[None, :, :]
    )
    pair_in = pair_in.reshape(pair_count, pair_width) + product(hot_table, rel_table)
    centred = pair_in - jnp.mean(pair_in, axis=-1, keepdims=True)
    inv_std = lax.rsqrt(jnp.mean(centred * centred, axis=-1, keepdims=True) + norm_eps)
    normed = centred * inv_std
    normed_bf = normed.astype(jnp.bfloat16)
    hidden_width = up_gate.shape[1] // 2
    both_pre = product(normed_bf, up_gate)
    up_pre = both_pre[:, :hidden_width]
    gate_pre = both_pre[:, hidden_width:]
    silu_value, silu_slope = gated_parts(gate_pre)
    hidden = (silu_value * up_pre).astype(jnp.bfloat16)
    pair_out = (pair_in + product(hidden, pair_down)).astype(jnp.bfloat16)
    cot_flat = cot_blk.reshape(pair_count, 2 * bin_count)
    symmetric = (
        cot_flat[:, bin_count:].astype(jnp.float32)
        + mirror_blk.reshape(pair_count, bin_count).astype(jnp.float32)
    ).astype(jnp.bfloat16)
    head_cot = jnp.concatenate([cot_flat[:, :bin_count], symmetric], axis=1)
    grad_out = product_right(head_cot, head_weight)
    grad_out_bf = grad_out.astype(jnp.bfloat16)
    grad_hidden = product_right(grad_out_bf, pair_down)
    grad_both = jnp.concatenate(
        [
            (grad_hidden * silu_value).astype(jnp.bfloat16),
            (grad_hidden * up_pre * silu_slope).astype(jnp.bfloat16),
        ],
        axis=1,
    )
    grad_normed = product_right(grad_both, up_gate)
    grad_in = grad_out + inv_std * (
        grad_normed
        - jnp.mean(grad_normed, axis=-1, keepdims=True)
        - normed * jnp.mean(grad_normed * normed, axis=-1, keepdims=True)
    )
    head_sum = product_left(pair_out, head_cot)
    down_sum = product_left(hidden, grad_out_bf)
    up_gate_sum = product_left(normed_bf, grad_both)
    rel_sum = lax.dot_general(
        one_hot.astype(jnp.float32),
        grad_in,
        (((0,), (0,)), ((), ())),
        precision=lax.Precision.HIGHEST,
        preferred_element_type=jnp.float32,
    )
    grad_tile = grad_in.reshape(n_rows, n_cols, pair_width)
    return (
        grad_tile.astype(jnp.bfloat16),
        jnp.sum(grad_tile, axis=1),
        jnp.sum(grad_tile, axis=0),
        up_gate_sum,
        down_sum,
        head_sum,
        rel_sum,
    )


def local(
    pair_repr,
    logit_cotangent,
    pair_mask,
    single_repr,
    token_index,
    pair_up,
    pair_gate,
    pair_down,
    head_weight,
    rel_table,
    proj_row,
    proj_col,
    single_gate,
    single_up,
    single_down,
):
    n_row = lax.axis_size("row")
    n_col = lax.axis_size("col")
    row_index = lax.axis_index("row")
    col_index = lax.axis_index("col")
    joint_index = row_index * n_col + col_index
    tile_rows, tile_cols, pair_width = pair_repr.shape
    bin_count = logit_cotangent.shape[2] // 2
    strip_len = single_repr.shape[0]
    tokens_all = strip_len * n_row * n_col
    hidden_width = pair_up.shape[1]
    saved_state = single_forward(single_repr, single_gate, single_up, single_down)
    updated = saved_state[7]
    row_piece = product(updated, proj_row).astype(jnp.bfloat16)
    col_piece = product(updated, proj_col).astype(jnp.bfloat16)
    row_proj = lax.all_gather(row_piece, "col", axis=0, tiled=True)
    col_whole = lax.all_gather(col_piece, ("row", "col"), axis=0, tiled=True)
    col_proj = lax.dynamic_slice_in_dim(col_whole, col_index * tile_cols, tile_cols, 0)
    masked = logit_cotangent * pair_mask[:, :, None].astype(jnp.bfloat16)
    distance_part = masked[:, :, bin_count:].reshape(tile_rows, tile_cols * bin_count)
    strips = lax.all_to_all(distance_part, "col", split_axis=0, concat_axis=1, tiled=True)
    columns = lax.all_to_all(strips, ("row", "col"), split_axis=1, concat_axis=0, tiled=True)
    returned = lax.all_to_all(columns, "col", split_axis=0, concat_axis=1, tiled=True)
    mirrored = returned.reshape(tile_cols, tile_rows, bin_count).transpose(1, 0, 2)
    up_gate = jnp.concatenate([pair_up, pair_gate], axis=1)
    row_pos = lax.dynamic_slice_in_dim(token_index, row_index * tile_rows, tile_rows, 0)
    col_pos = lax.dynamic_slice_in_dim(token_index, col_index * tile_cols, tile_cols, 0)
    block_count = 4
    block_rows = tile_rows // block_count

    def block_step(running, inputs):
        pair_blk, cot_blk, mirror_blk, row_blk, pos_blk = inputs
        grad_blk, row_sum, col_sum, up_gate_sum, down_sum, head_sum, rel_sum = pair_block(
            pair_blk,
            cot_blk,
            mirror_blk,
            row_blk,
            col_proj,
            pos_blk,
            col_pos,
            rel_table,
            up_gate,
            pair_down,
            head_weight,
        )
        running = (
            running[0] + col_sum,
            running[1] + up_gate_sum,
            running[2] + down_sum,
            running[3] + head_sum,
            running[4] + rel_sum,
        )
        return (running, (grad_blk, row_sum))

    initial = (
        jnp.zeros((tile_cols, pair_width), jnp.float32),
        jnp.zeros(up_gate.shape, jnp.float32),
        jnp.zeros(pair_down.shape, jnp.float32),
        jnp.zeros(head_weight.shape, jnp.float32),
        jnp.zeros(rel_table.shape, jnp.float32),
    )
    sliced = (
        pair_repr.reshape(block_count, block_rows, tile_cols, pair_width),
        masked.reshape(block_count, block_rows, tile_cols, 2 * bin_count),
        mirrored.reshape(block_count, block_rows, tile_cols, bin_count),
        row_proj.reshape(block_count, block_rows, pair_width),
        row_pos.reshape(block_count, block_rows),
    )
    sums_out, blocks_out = lax.scan(block_step, initial, sliced)
    col_total, up_gate_sum, down_sum, head_sum, rel_sum = sums_out
    grad_blocks, row_sums = blocks_out
    pair_grad = grad_blocks.reshape(tile_rows, tile_cols, pair_width)
    row_tile = row_sums.reshape(tile_rows, pair_width)
    row_part = lax.psum_scatter(
        row_tile.astype(jnp.bfloat16), "col", scatter_dimension=0, tiled=True
    )
    col_summed = lax.psum(col_total.astype(jnp.bfloat16), "row")
    col_every = lax.all_gather(col_summed, "col", axis=0, tiled=True)
    col_bf = lax.dynamic_slice_in_dim(col_every, joint_index * strip_len, strip_len, 0)
    single_cot = product_right(row_part, proj_row) + product_right(col_bf, proj_col)
    prow_sum = product_left(updated, row_part)
    pcol_sum = product_left(updated, col_bf)
    grad_source, grad_bf, grad_gate, grad_up = single_backward(
        single_cot, saved_state, single_gate, single_up, single_down
    )
    normed_bf = saved_state[2]
    hidden = saved_state[6]
    stacked = local_weight_sums(normed_bf, grad_bf, grad_gate, grad_up, hidden)
    summed = lax.psum(stacked, ("row", "col"))
    share_len = summed.shape[2] // (n_row * n_col)
    own_share = lax.dynamic_slice_in_dim(summed, joint_index * share_len, share_len, 2)
    totals = lax.psum(
        (up_gate_sum, down_sum, head_sum, rel_sum, prow_sum, pcol_sum), ("row", "col")
    )
    grad_scale = 1.0 / tokens_all
    return (
        pair_grad,
        grad_source.astype(jnp.bfloat16),
        totals[0][:, :hidden_width] * grad_scale,
        totals[0][:, hidden_width:] * grad_scale,
        totals[1] * grad_scale,
        totals[2] * grad_scale,
        totals[3] * grad_scale,
        totals[4] * grad_scale,
        totals[5] * grad_scale,
        own_share[0] * grad_scale,
        own_share[1] * grad_scale,
        jnp.transpose(own_share[2]) * grad_scale,
    )


def solution(mesh):
    placed = (
        P("row", "col", None),
        P("row", "col", None),
        P("row", "col"),
        P(("row", "col"), None),
        P(),
        P(),
        P(),
        P(),
        P(),
        P(),
        P(),
        P(),
        P(),
        P(),
        P(),
    )
    return jax.shard_map(
        local,
        mesh=mesh,
        in_specs=placed,
        out_specs=(
            P("row", "col", None),
            P(("row", "col"), None),
            P(),
            P(),
            P(),
            P(),
            P(),
            P(),
            P(),
            P(None, ("row", "col")),
            P(None, ("row", "col")),
            P(("row", "col"), None),
        ),
        check_vma=False,
    )
```

profile of v0, /device:TPU:1, one launch (start us, length us, event | category | flops | bytes accessed | tf_op | source)
XLA Modules:
  0.0 706.4 jit_solution(2724310889177387201)
XLA Ops:
  8.2 3.4 broadcast_multiply_fusion.3
  11.6 2.3 slice.44
  13.9 2.5 all_to_all.36
  16.3 22.8 %all_to_all.48 = bf16[16,8,4096]{2,1,0:T(8,128)(2,1)} all-to-all(bf16[16,8,4096]{2,1,0:T(8,128)(2,1)} %all_to_all.36), channel_id=1, replica_groups=mesh['row'=8,'col'=16] {'col'}, dimensions={0} | all-to-all | bytes 2097152 | tf_op jit(solution)/shard_map/all_to_all | solution.py:185
  39.2 9.1 %all-to-all-start.1 = ((bf16[8,128,512]{2,0,1:T(8,128)(2,1)}), bf16[8,128,512]{2,0,1:T(8,128)(2,1)}, u32[]{:S(2)}, u32[]{:S(2)}) async-start(bf16[8,128,512]{2,0,1:T(8,128)(2,1)} %bitcast.2), calls=%async_computation.1 | async-start | bytes 2097152 | tf_op jit(solution)/shard_map/all_to_all | solution.py:186
  53.5 13.4 %all-to-all-done.1 = bf16[8,128,512]{2,0,1:T(8,128)(2,1)} async-done(((bf16[8,128,512]{2,0,1:T(8,128)(2,1)}), bf16[8,128,512]{2,0,1:T(8,128)(2,1)}, u32[]{:S(2)}, u32[]{:S(2)}) %all-to-all-start.1) | async-done | bytes 1048608 | tf_op jit(solution)/shard_map/all_to_all | solution.py:186
  66.9 5.1 all-to-all-start.2
  72.4 27.1 %all_gather.9 = bf16[128,128]{1,0:T(8,128)(2,1)} all-gather(bf16[8,128]{1,0:T(8,128)(2,1)S(1)} %convolution_convert_fusion.1), channel_id=1, replica_groups=mesh['row'=8,'col'=16] {'col'}, dimensions={0}, use_global_device_ids=true | all-gather | bytes 34816 | tf_op jit(solution)/shard_map/all_gather | solution.py:180
  99.7 173.0 %all_gather.10 = bf16[1024,128]{1,0:T(8,128)(2,1)S(1)} all-gather(bf16[8,128]{1,0:T(8,128)(2,1)S(1)} %convolution_convert_fusion), channel_id=1, replica_groups=mesh['row'=8,'col'=16] {'row','col'}, dimensions={0}, use_global_device_ids=true | all-gather | bytes 264192 | tf_op jit(solution)/shard_map/all_gather | solution.py:181
  275.1 2.1 reshape.165
  277.2 136.8 %while.23 = (s32[]{:T(128)}, f32[64,128]{1,0:T(8,128)}, f32[128,1024]{1,0:T(8,128)}, f32[512,128]{1,0:T(8,128)}, f32[128,128]{1,0:T(8,128)}, /*index=5*/f32[65,1...) while((s32[]{:T(128)}, f32[64,128]{1,0:T(8,128)}, ...), condition=%wide.region_8.9_spmd.clone, body=%wide.region_1.8_spmd.clone.sunk | while | flops 2833191168 | bytes 105293408 | solution.py:233
  281.6 1.8 fusion.126
  285.9 3.5 multiply_convert_fusion.7
  289.4 2.5 fusion.127
  292.0 1.9 bitcast_reduce_fusion.2
  294.8 3.9 fusion.129
  298.6 3.4 convolution_add_fusion.9
  302.1 3.9 fusion.128
  307.4 2.6 convolution_add_fusion.10
  315.2 1.8 fusion.126
  319.4 3.5 multiply_convert_fusion.7
  322.9 2.5 fusion.127
  325.5 1.9 bitcast_reduce_fusion.2
  328.3 3.9 fusion.129
  332.2 3.5 convolution_add_fusion.9
  335.6 3.9 fusion.128
  341.8 2.7 convolution_add_fusion.10
  349.6 1.8 fusion.126
  353.8 3.5 multiply_convert_fusion.7
  357.4 2.5 fusion.127
  360.0 1.9 bitcast_reduce_fusion.2
  362.7 3.9 fusion.129
  366.6 3.5 convolution_add_fusion.9
  370.1 3.9 fusion.128
  376.2 2.7 convolution_add_fusion.10
  388.2 3.5 multiply_convert_fusion.7
  391.8 2.5 fusion.127
  394.4 1.9 bitcast_reduce_fusion.2
  397.1 3.9 fusion.129
  401.0 3.5 convolution_add_fusion.9
  404.5 3.9 fusion.128
  410.6 2.7 convolution_add_fusion.10
  414.0 49.4 %all-reduce = bf16[128,128]{1,0:T(8,128)(2,1)S(1)} all-reduce(bf16[128,128]{1,0:T(8,128)(2,1)} %bitcast.131), channel_id=2, replica_groups=mesh['row'=8,'col'=16] {'col'}, use_global_device_ids=true, to_apply=%region_9.10.clone | all-reduce | flops 16384 | bytes 65536
  466.8 29.8 %psum.56 = bf16[64,128]{1,0:T(8,128)(2,1)S(1)} all-reduce(bf16[64,128]{1,0:T(8,128)(2,1)S(1)} %convert_element_type.121), channel_id=1, replica_groups=mesh['row'=8,'col'=16] {'row'}, use_global_device_ids=true, to_apply=%region_10.11 | all-reduce | flops 8192 | bytes 32768 | tf_op jit(solution)/shard_map/psum | solution.py:241
  496.6 28.2 %all_gather.11 = bf16[1024,128]{1,0:T(8,128)(2,1)S(1)} all-gather(bf16[64,128]{1,0:T(8,128)(2,1)S(1)} %psum.56), channel_id=1, replica_groups=mesh['row'=8,'col'=16] {'col'}, dimensions={0}, use_global_device_ids=true | all-gather | bytes 278528 | tf_op jit(solution)/shard_map/all_gather | solution.py:242
  530.3 3.5 pad_maximum_fusion.8
  534.5 63.7 %psum.60 = f32[65,128]{1,0:T(8,128)S(1)} all-reduce(f32[65,128]{1,0:T(8,128)S(1)} %copy-done.10), channel_id=1, replica_groups=mesh['row'=8,'col'=16] {'row','col'}, use_global_device_ids=true, to_apply=%region_15.16 | all-reduce | flops 8320 | bytes 66560 | tf_op jit(solution)/shard_map/psum | solution.py:256
  600.6 92.2 %all-reduce.4.cloned.1.call-done = (f32[128,1024]{1,0:T(8,128)}, f32[512,128]{1,0:T(8,128)}, f32[128,128]{1,0:T(8,128)}, f32[384,128]{1,0:T(8,128)}, f32[384,128]{1,0:T(8,128)}, /*index=5*/f32[3,384,1536]{2,1,0:T(8,128)}) async-done(((f32[128,1024]{1,0:T(8,128)}, f32[512,128]{1,0:T(8,128)}, f32[128,128]{1,0:T(8,128)}, f32[384,128]{1,0:T(8,128)}, f32[384,128]{1,0:T(8,128)}, ...) | async-done | bytes 8323088 | tf_op jit(solution)/shard_map/psum | solution.py:256
  (323 shorter events, 70.1 us)
Async XLA Ops:
  7.2 45.4 %copy-start = (bf16[384,1536]{1,0:T(8,128)(2,1)S(1)}, bf16[384,1536]{1,0:T(8,128)(2,1)}, u32[]{:S(2)}) copy-start(bf16[384,1536]{1,0:T(8,128)(2,1)} %param.30) | copy-start | bytes 3538948
  16.3 33.7 %copy-start.38 = (u32[128]{0:T(128)S(1)}, u32[128]{0:T(128)}, u32[]{:S(2)}) copy-start(u32[128]{0:T(128)} %constant.89) | copy-start | bytes 1540
  16.3 34.9 %copy-start.19 = (bf16[8,384]{1,0:T(8,128)(2,1)S(1)}, bf16[8,384]{1,0:T(8,128)(2,1)}, u32[]{:S(2)}) copy-start(bf16[8,384]{1,0:T(8,128)(2,1)} %param.20) | copy-start | bytes 18436
  16.3 35.0 %copy-start.6 = (bf16[384,1536]{1,0:T(8,128)(2,1)S(1)}, bf16[384,1536]{1,0:T(8,128)(2,1)}, u32[]{:S(2)}) copy-start(bf16[384,1536]{1,0:T(8,128)(2,1)} %param.29) | copy-start | bytes 3538948
  39.2 27.7 %all-to-all-start.1 = ((bf16[8,128,512]{2,0,1:T(8,128)(2,1)}), bf16[8,128,512]{2,0,1:T(8,128)(2,1)}, u32[]{:S(2)}, u32[]{:S(2)}) async-start(bf16[8,128,512]{2,0,1:T(8,128)(2,1)} %bitcast.2), calls=%async_computation.1 | async-start | bytes 2097152 | tf_op jit(solution)/shard_map/all_to_all | solution.py:186
  51.4 20.6 %copy-start.4 = (bf16[1536,384]{1,0:T(8,128)(2,1)S(1)}, bf16[1536,384]{1,0:T(8,128)(2,1)}, u32[]{:S(2)}) copy-start(bf16[1536,384]{1,0:T(8,128)(2,1)} %param.31) | copy-start | bytes 3538948
  52.6 19.7 %copy-start.21 = (bf16[384,128]{1,0:T(8,128)(2,1)S(1)}, bf16[384,128]{1,0:T(8,128)(2,1)}, u32[]{:S(2)}) copy-start(bf16[384,128]{1,0:T(8,128)(2,1)} %param.27) | copy-start | bytes 294916
  52.6 47.0 %copy-start.22 = (bf16[384,128]{1,0:T(8,128)(2,1)S(1)}, bf16[384,128]{1,0:T(8,128)(2,1)}, u32[]{:S(2)}) copy-start(bf16[384,128]{1,0:T(8,128)(2,1)} %param.28) | copy-start | bytes 294916
  53.5 219.8 %copy-start.24 = (bf16[8,1536]{1,0:T(8,128)(2,1)}, bf16[8,1536]{1,0:T(8,128)(2,1)S(1)}, u32[]{:S(2)}) copy-start(bf16[8,1536]{1,0:T(8,128)(2,1)S(1)} %get-tuple-element.319) | copy-start | bytes 73732
  53.5 219.8 %copy-start.29 = (bf16[128,512]{1,0:T(8,128)(2,1)S(1)}, bf16[128,512]{1,0:T(8,128)(2,1)}, u32[]{:S(2)}) copy-start(bf16[128,512]{1,0:T(8,128)(2,1)} %param.23) | copy-start | bytes 393220
  53.5 219.8 %copy-start.30 = (bf16[128,512]{1,0:T(8,128)(2,1)S(1)}, bf16[128,512]{1,0:T(8,128)(2,1)}, u32[]{:S(2)}) copy-start(bf16[128,512]{1,0:T(8,128)(2,1)} %param.22) | copy-start | bytes 393220
  66.9 206.4 %all-to-all-start.2 = ((bf16[16,64,512]{2,1,0:T(8,128)(2,1)}), bf16[16,64,512]{2,1,0:T(8,128)(2,1)}, u32[]{:S(2)}, u32[]{:S(2)}) async-start(bf16[16,64,512]{2,1,0:T(8,128)(2,1)} %bitcast.4), calls=%async_computation.2 | async-start | bytes 2097152 | tf_op jit(solution)/shard_map/all_to_all | solution.py:187
  72.0 620.9 %all-reduce.4.cloned.1.call-start = ((), (), s32[]{:S(2)}) async-start(), calls=%async_computation.3 | async-start | bytes 16646144 | tf_op jit(solution)/shard_map/psum | solution.py:256
  72.3 204.9 %copy-start.28 = (bf16[8,384]{1,0:T(8,128)(2,1)}, bf16[8,384]{1,0:T(8,128)(2,1)S(1)}, u32[]{:S(2)}) copy-start(bf16[8,384]{1,0:T(8,128)(2,1)S(1)} %fusion.24) | copy-start | bytes 18436
  278.5 6.6 copy-start.2
  285.9 6.1 copy-start.1
  306.7 4.0 copy-start.35
  306.7 4.0 copy-start.37
  312.0 6.6 copy-start.2
  319.4 6.2 copy-start.1
  332.2 3.5 copy-start.40
  340.3 4.2 copy-start.12
  340.3 4.8 copy-start.35
  340.3 4.8 copy-start.37
  346.4 6.6 copy-start.2
  353.8 6.1 copy-start.1
  366.6 3.5 copy-start.14
  366.6 3.5 copy-start.40
  374.7 4.2 copy-start.12
  374.7 4.8 copy-start.35
  374.7 4.8 copy-start.37
  380.8 6.6 copy-start.2
  388.2 6.1 copy-start.1
  401.0 3.5 copy-start.40
  409.1 4.2 copy-start.12
  409.1 4.8 copy-start.35
  409.1 4.8 copy-start.37
  413.9 114.7 %copy-start.5 = (bf16[1536,384]{1,0:T(8,128)(2,1)S(1)}, bf16[1536,384]{1,0:T(8,128)(2,1)}, u32[]{:S(2)}) copy-start(bf16[1536,384]{1,0:T(8,128)(2,1)} %param.31) | copy-start | bytes 3538948
  414.0 114.7 %copy-start.18 = (f32[8,1536]{1,0:T(8,128)S(1)}, f32[8,1536]{1,0:T(8,128)}, u32[]{:S(2)}) copy-start(f32[8,1536]{1,0:T(8,128)} %copy-done.17) | copy-start | bytes 147460
  414.0 114.7 %copy-start.25 = (f32[8,1536]{1,0:T(8,128)S(1)}, f32[8,1536]{1,0:T(8,128)}, u32[]{:S(2)}) copy-start(f32[8,1536]{1,0:T(8,128)} %get-tuple-element.320) | copy-start | bytes 147460
  524.7 4.4 copy-start.20
  524.7 4.4 copy-start.33
  533.8 64.5 %copy-start.7 = (bf16[384,1536]{1,0:T(8,128)(2,1)S(1)}, bf16[384,1536]{1,0:T(8,128)(2,1)}, u32[]{:S(2)}) copy-start(bf16[384,1536]{1,0:T(8,128)(2,1)} %param.29) | copy-start | bytes 3538948
  692.8 3.7 copy-start.16
  692.8 4.6 copy-start.23
  692.8 5.3 copy-start.31
  692.8 5.9 copy-start.26
  692.8 5.9 copy-start.27
  (48 other events, 94.3 us)
Sparse Core Ops, SparseCore 0:
  533.9 158.8 all-reduce.3
where the time goes:
time: 709 us; the launch traced here: 706 us
  blocking collectives  394 us (56%)
  waiting for transfers between devices  106 us (15%)
  matrix products  105 us (15%)
  local copies, waits for them, and re-layouts  37.5 us (5%)
  other arithmetic  34 us (5%)
  between operations  15 us (2%)
  starting transfers between devices  14.2 us (2%)
    all_gather x1, blocking collectives, local(): col_whole = lax.all_gather(col_piece, ('row', 'col'), axis=0, tiled=True)  173 us
    psum x1, waiting for transfers between devices, local(): lax.psum((up_gate_sum, down_sum, head_sum, rel_sum, prow_sum, pcol_sum),...  92.2 us
    psum x1, blocking collectives, local(): lax.psum((up_gate_sum, down_sum, head_sum, rel_sum, prow_sum, pcol_sum),...  63.7 us
    dot_general x17, matrix products, product_left(): lax.dot_general(matrix_a, matrix_b, (((0,), (0,)), ((), ())), preferred_e...  50.4 us
    unnamed x1, blocking collectives  49.4 us
    psum x1, blocking collectives, local(): col_summed = lax.psum(col_total.astype(jnp.bfloat16), 'row')  29.8 us
    dot_general x17, matrix products, product_right(): lax.dot_general(matrix_a, matrix_b, (((1,), (1,)), ((), ())), preferred_e...  29.4 us
    all_gather x1, blocking collectives, local(): col_every = lax.all_gather(col_summed, 'col', axis=0, tiled=True)  28.2 us
  transfers between devices with their start and end apart: 3, of which 2 were waited for; matrix products, arithmetic and copies ran while one was open for 1% of the time, Pallas kernels for 0%

commit v1 on v0

v1 whole, which is shorter than its diff:
```python
import jax
import jax.numpy as jnp
from jax import lax
from jax.experimental import pallas as pl
from jax.experimental.pallas import tpu as pltpu
from jax.sharding import PartitionSpec as P

F = jnp.float32
B = jnp.bfloat16
MESH = pl.DeviceIdType.MESH
NR, NC = 8, 16
EPS = 1e-05
BR = 32
SHARE = 112


def mm(a, b):
    return lax.dot_general(a, b, (((1,), (0,)), ((), ())), preferred_element_type=F)


def nt(a, b):
    return lax.dot_general(a, b, (((1,), (1,)), ((), ())), preferred_element_type=F)


def tn(a, b):
    return lax.dot_general(a, b, (((0,), (0,)), ((), ())), preferred_element_type=F)


def sigmoid(v):
    return 0.5 * jnp.tanh(0.5 * v) + 0.5


def local_wait(ref, sem):
    pltpu.make_async_copy(ref, ref, sem).wait()


def kernel(
    pair_hbm, cot_hbm, mask, single, tok, tok_s, up, gate, down, head, rel, prow, pcol,
    sgate, sup, sdown,
    og, osg, oup, ogate, odown, ohead, orel, opr, opc, osgate, osup, osdown,
    pairv, cotv, ogv, lo, hi, pos, srel, smask, tbuf, sendm, mirb, sb, rowp, colp,
    arow, acol, aug, adn, ahd, arl, ws, wr, w2, w3, rr, cr, tb, cots,
    in_sem, out_sem, msend, mrecv, gsend, grecv, csend, crecv, hsend, hrecv,
    p1s, p1r, rs1, rr1, cs1, cr1, p2s, p2r, t2s, t2r, p3s, p3r, t3s, t3r,
):
    r = lax.axis_index("row")
    c = lax.axis_index("col")
    joint = r * NC + c
    diag = c // 2 == r

    cot_in = pltpu.make_async_copy(cot_hbm, cotv, in_sem.at[0])
    cot_in.start()
    pair_in = pltpu.make_async_copy(pair_hbm, pairv, in_sem.at[1])
    pair_in.start()

    bar = pltpu.get_barrier_semaphore()
    for d in range(1, NC):
        pl.semaphore_signal(bar, inc=1, device_id=(r, lax.rem(c + d, NC)), device_id_type=MESH)
    for d in range(1, NR):
        pl.semaphore_signal(bar, inc=1, device_id=(lax.rem(r + d, NR), c), device_id_type=MESH)
    for h in range(2):
        @pl.when(jnp.logical_not(jnp.logical_and(diag, c % 2 == h)))
        def _():
            pl.semaphore_signal(bar, inc=1, device_id=(c // 2, 2 * r + h), device_id_type=MESH)

    lane = lax.broadcasted_iota(jnp.int32, (64, 128), 1)
    trow = jnp.broadcast_to(tok[pl.ds(c // 2, 1), :].astype(F), (128, 128))
    pos[...] = jnp.transpose(trow)
    e = pos[pl.ds((c % 2) * 64, 64), :].astype(jnp.int32) + lane - 32
    big = jnp.int32(1 << 20)
    lo[...] = jnp.where(lane == 0, -big, jnp.where(lane > 64, big, e))
    hi[...] = jnp.where(lane == 64, big, jnp.where(lane > 64, -big, e))
    srel[...] = jnp.zeros_like(srel)
    srel[0:65, :] = rel[...].astype(F)
    mt = jnp.transpose(mask[...].astype(F))
    for b in range(4):
        smask[b] = mt[:, b * 32:(b + 1) * 32]
    for a in (acol, aug, adn, ahd, arl):
        a[...] = jnp.zeros_like(a)

    src = single[...].astype(F)
    inv_rms = lax.rsqrt(jnp.mean(src * src, axis=-1, keepdims=True) + EPS)
    normed = src * inv_rms
    nbf = normed.astype(B)
    s_gate = mm(nbf, sgate[...])
    s_up = mm(nbf, sup[...])
    s_sig = sigmoid(s_gate)
    s_silu = s_gate * s_sig
    s_hid = (s_silu * s_up).astype(B)
    updated = src + mm(s_hid, sdown[...])
    for k in range(3):
        ks = slice(k * 128, (k + 1) * 128)
        sb[r, c, k] = jnp.concatenate([src[:, ks], updated[:, ks]], axis=0).astype(B)

    pl.semaphore_wait(bar, NC + NR - jnp.where(diag, 1, 0))

    def col_copies(src_ref, dst_ref, ss, rs):
        return [
            pltpu.make_async_remote_copy(
                src_ref=src_ref(lax.rem(c + d, NC)), dst_ref=dst_ref, send_sem=ss.at[d], recv_sem=rs.at[d],
                device_id=(r, lax.rem(c + d, NC)), device_id_type=MESH,
            )
            for d in range(1, NC)
        ]

    def row_copies(src_ref, dst_ref, ss, rs):
        return [
            pltpu.make_async_remote_copy(
                src_ref=src_ref(lax.rem(r + d, NR)), dst_ref=dst_ref, send_sem=ss.at[d], recv_sem=rs.at[d],
                device_id=(lax.rem(r + d, NR), c), device_id_type=MESH,
            )
            for d in range(1, NR)
        ]

    def start(copies):
        for cp in copies:
            cp.start()

    def wait(copies):
        for cp in copies:
            cp.wait()

    strips = col_copies(lambda j: sb.at[r, c], sb.at[r, c], gsend, grecv)
    start(strips)

    cot_in.wait()
    half_lane = lax.broadcasted_iota(jnp.int32, (16, 128), 1) < 64
    for h in range(2):
        @pl.loop(0, 2)
        def _(b):
            p0 = h * 64 + b * 32
            sm = smask[2 * h + b]
            for i in range(32):
                v = cotv[p0 + i].astype(F) * jnp.broadcast_to(sm[:, i:i + 1], (64, 128))
                cotv[p0 + i] = v.astype(B)
                for t in range(2):
                    first = pltpu.roll(v[32 * t:32 * t + 16], 64, 1)
                    second = v[32 * t + 16:32 * t + 32]
                    at = pl.multiple_of((b * 32 + i) * 16, 16)
                    tbuf[t, pl.ds(at, 16), :] = jnp.where(half_lane, first, second)
        for t in range(2):
            for k in range(16):
                sendm[t, h, k] = tbuf[t, pl.ds(k, 64, stride=16), :].astype(B)
    for t in range(2):
        for h in range(2):
            own = jnp.logical_and(diag, c % 2 == h)

            @pl.when(own)
            def _():
                pltpu.make_async_copy(sendm.at[t, h], mirb.at[c % 2, t], mrecv.at[c % 2, t]).start()

            @pl.when(jnp.logical_not(own))
            def _():
                pltpu.make_async_remote_copy(
                    src_ref=sendm.at[t, h], dst_ref=mirb.at[c % 2, t], send_sem=msend.at[t, h],
                    recv_sem=mrecv.at[c % 2, t], device_id=(c // 2, 2 * r + h), device_id_type=MESH,
                ).start()

    wait(strips)
    row_u = [sb[r, :, k].astype(F)[:, 8:].reshape(128, 128).astype(B) for k in range(3)]
    rowp[...] = sum(mm(row_u[k], prow[k * 128:(k + 1) * 128]) for k in range(3)).astype(B).astype(F)

    cols = row_copies(lambda j: colp, colp, csend, crecv)

    @pl.when(diag)
    def _():
        full = sum(mm(row_u[k], pcol[k * 128:(k + 1) * 128]) for k in range(3))
        pos[...] = full
        colp[...] = pos[pl.ds((c % 2) * 64, 64), :].astype(B)
        start(cols)

    spread = row_copies(lambda j: sb.at[r], sb.at[r], hsend, hrecv)
    start(spread)

    @pl.when(jnp.logical_not(diag))
    def _():
        for d in range(1, NR):
            @pl.when(lax.rem(c // 2 + d, NR) == r)
            def _():
                local_wait(colp, crecv.at[d])

    @pl.when(diag)
    def _():
        for cp in cols:
            cp.wait_send()

    pair_in.wait()
    lane3 = lax.broadcasted_iota(jnp.int32, (1, 1, 128), 2)

    @pl.loop(0, 4)
    def _(b):
        s = b % 2
        t = b // 2
        i0 = pl.multiple_of(s * 64 + t * 32, 32)
        local_wait(mirb.at[s, t], mrecv.at[s, t])
        m = BR * 64
        hots = []
        for k in range(BR):
            at = tok_s[r * 128 + i0 + k]
            hots.append(jnp.where((lo[...] <= at) & (hi[...] >= at), F(1), F(0)).astype(B))
        hot = jnp.concatenate(hots, axis=0)
        x = (
            pairv[pl.ds(i0, BR)].astype(F)
            + rowp[pl.ds(i0, BR)][:, None, :]
            + colp[...].astype(F)[None]
        )
        x = x.reshape(m, 128) + mm(hot, srel[...].astype(B))
        cen = x - jnp.mean(x, axis=-1, keepdims=True)
        inv = lax.rsqrt(jnp.mean(cen * cen, axis=-1, keepdims=True) + EPS)
        nm = cen * inv
        nb = nm.astype(B)
        u = mm(nb, up[...])
        g = mm(nb, gate[...])
        sg = sigmoid(g)
        si = g * sg
        hid = (si * u).astype(B)
        po = (x + mm(hid, down[...])).astype(B)
        mv = mirb[s, t].astype(F)
        first = pltpu.roll(mv.reshape(1024, 128), 64, 1).reshape(16, 64, 128)
        mir = jnp.where(lane3 >= 64, jnp.concatenate([first, mv], axis=0), 0.0)
        hc = (cotv[pl.ds(i0, BR)].astype(F) + mir).astype(B).reshape(m, 128)
        go = nt(hc, head[...])
        gb = go.astype(B)
        gh = nt(gb, down[...])
        gu = (gh * si).astype(B)
        gg = (gh * u * (sg + si * (1.0 - sg))).astype(B)
        gn = nt(gu, up[...]) + nt(gg, gate[...])
        gx = go + inv * (
            gn - jnp.mean(gn, axis=-1, keepdims=True) - nm * jnp.mean(gn * nm, axis=-1, keepdims=True)
        )
        gt = gx.reshape(BR, 64, 128)
        gxb = gx.astype(B)
        ogv[pl.ds(i0, BR)] = gxb.reshape(BR, 64, 128)
        pltpu.make_async_copy(ogv.at[pl.ds(i0, BR)], og.at[pl.ds(i0, BR)], out_sem.at[b]).start()
        arow[pl.ds(i0, BR)] = jnp.sum(gt, axis=1)
        acol[...] += jnp.sum(gt, axis=0)
        aug[:, :512] += tn(nb, gu)
        aug[:, 512:] += tn(nb, gg)
        adn[...] += tn(gb, hid)
        ahd[...] += tn(po, hc)
        arl[...] += tn(hot, gxb)

    for k in range(8):
        ws[k * 128:(k + 1) * 128] = aug[:, k * 128:(k + 1) * 128].astype(B)
    for k in range(4):
        ws[1024 + k * 128:1152 + k * 128] = adn[:, k * 128:(k + 1) * 128].astype(B)
    ws[1536:1664] = ahd[...].astype(B)
    ws[1664:1792] = arl[...].astype(B)
    share = lambda j: pl.ds(pl.multiple_of(j * SHARE, 16), SHARE)
    strip = lambda j: pl.ds(pl.multiple_of(j * 8, 8), 8)
    s_row = col_copies(lambda j: arow.at[strip(j)], rr.at[c], rs1, rr1)
    s_col = row_copies(lambda j: acol.at[strip(j)], cr.at[r], cs1, cr1)
    s_w = col_copies(lambda j: ws.at[share(j)], wr.at[c], p1s, p1r)
    start(s_row)
    start(s_col)
    start(s_w)
    wr[c] = ws[share(c)]
    rr[c] = arow[strip(c)]
    cr[r] = acol[strip(r)]

    wait(spread)
    s_all = [sb[:, :, k].astype(F)[:, :, :8].reshape(1024, 128) for k in range(3)]
    u_all = jnp.concatenate(
        [sb[:, :, k].astype(F)[:, :, 8:].reshape(1024, 128).astype(B) for k in range(3)], axis=1
    )
    s_all = jnp.concatenate(s_all, axis=1)
    nb_all = (s_all * lax.rsqrt(jnp.mean(s_all * s_all, axis=-1, keepdims=True) + EPS)).astype(B)
    picks = lax.broadcasted_iota(jnp.int32, (128, 1536), 1)
    unit = lax.broadcasted_iota(jnp.int32, (128, 1536), 0)
    pick = jnp.where((picks == joint * 12 + unit) & (unit < 12), F(1), F(0)).astype(B)
    own_gate = nt(pick, sgate[...]).astype(B)
    own_up = nt(pick, sup[...]).astype(B)
    own_down = mm(pick, sdown[...]).astype(B)
    g12 = nt(nb_all, own_gate)
    u12 = nt(nb_all, own_up)
    sg12 = sigmoid(g12)
    si12 = g12 * sg12
    slope12 = u12 * (sg12 + si12 * (1.0 - sg12))
    h12 = (si12 * u12).astype(B)

    wait(s_row)
    wait(s_col)
    row_own = rr[0]
    for k in range(1, NC):
        row_own = row_own + rr[k]
    col_own = cr[0]
    for k in range(1, NR):
        col_own = col_own + cr[k]
    tb[c, r] = jnp.concatenate([row_own, col_own], axis=0).astype(B)
    t2 = row_copies(lambda j: tb.at[c, r], tb.at[c, r], t2s, t2r)
    start(t2)
    wait(s_w)
    w = wr[0].astype(F)
    for k in range(1, NC):
        w = w + wr[k].astype(F)
    w2[r] = w.astype(B)
    s2 = row_copies(lambda j: w2.at[r], w2.at[r], p2s, p2r)
    start(s2)
    wait(t2)
    t3 = col_copies(lambda j: tb.at[c], tb.at[c], t3s, t3r)
    start(t3)
    wait(s2)
    w = w2[0].astype(F)
    for k in range(1, NR):
        w = w + w2[k].astype(F)
    w3[share(c)] = w.astype(B)
    s3 = col_copies(lambda j: w3.at[share(c)], w3.at[share(c)], p3s, p3r)
    start(s3)

    scale = 1.0 / 1024
    wait(t3)
    tf = tb[...].astype(F)
    row_all = jnp.swapaxes(tf[:, :, :8], 0, 1).reshape(1024, 128).astype(B)
    col_all = tf[:, :, 8:].reshape(1024, 128).astype(B)
    cot_all = nt(row_all, prow[...]) + nt(col_all, pcol[...])
    cots[...] = cot_all
    cb = cot_all.astype(B)
    gsh = nt(cb, own_down)
    gsu = (gsh * si12).astype(B)
    gsg = (gsh * slope12).astype(B)
    osgate[...] = tn(nb_all, gsg)[:, :12] * scale
    osup[...] = tn(nb_all, gsu)[:, :12] * scale
    osdown[...] = tn(h12, cb)[:12] * scale
    opr[...] = tn(u_all, row_all) * scale
    opc[...] = tn(u_all, col_all) * scale
    c8 = cots[pl.ds(pl.multiple_of(joint * 8, 8), 8), :]
    g8 = nt(c8.astype(B), sdown[...])
    gu8 = (g8 * s_silu).astype(B)
    gg8 = (g8 * s_up * (s_sig + s_silu * (1.0 - s_sig))).astype(B)
    gn8 = nt(gg8, sgate[...]) + nt(gu8, sup[...])
    osg[...] = (
        c8 + inv_rms * (gn8 - normed * jnp.mean(gn8 * normed, axis=-1, keepdims=True))
    ).astype(B)

    wait(s3)
    for k in range(4):
        ks = slice(k * 128, (k + 1) * 128)
        oup[:, ks] = w3[k * 128:(k + 1) * 128].astype(F) * scale
        ogate[:, ks] = w3[512 + k * 128:640 + k * 128].astype(F) * scale
        odown[ks, :] = jnp.transpose(w3[1024 + k * 128:1152 + k * 128].astype(F)) * scale
    ohead[...] = w3[1536:1664].astype(F) * scale
    orel[...] = (w3[1664:1792].astype(F) * scale)[:65]

    for t in range(2):
        for h in range(2):
            @pl.when(jnp.logical_not(jnp.logical_and(diag, c % 2 == h)))
            def _():
                local_wait(sendm.at[t, h], msend.at[t, h])
    for b in range(4):
        i0 = (b % 2) * 64 + (b // 2) * 32
        pltpu.make_async_copy(ogv.at[pl.ds(i0, BR)], og.at[pl.ds(i0, BR)], out_sem.at[b]).wait()


def local(
    pair_repr, logit_cotangent, pair_mask, single_repr, token_index, pair_up, pair_gate, pair_down,
    head_weight, rel_table, proj_row, proj_col, single_gate, single_up, single_down,
):
    S = lambda shape, dtype=F: jax.ShapeDtypeStruct(shape, dtype)
    V = pl.BlockSpec(memory_space=pltpu.VMEM)
    H = pl.BlockSpec(memory_space=pl.ANY)
    vm = lambda *shape: pltpu.VMEM(shape, F)
    vb = lambda *shape: pltpu.VMEM(shape, B)
    dma = lambda *shape: pltpu.SemaphoreType.DMA(shape)
    return pl.pallas_call(
        kernel,
        out_shape=(
            S((128, 64, 128), B), S((8, 384), B), S((128, 512)), S((128, 512)), S((512, 128)),
            S((128, 128)), S((65, 128)), S((384, 128)), S((384, 128)), S((384, 12)), S((384, 12)),
            S((12, 384)),
        ),
        in_specs=[H, H, V, V, V, pl.BlockSpec(memory_space=pltpu.SMEM)] + [V] * 10,
        out_specs=[H] + [V] * 11,
        scratch_shapes=[
            vb(128, 64, 128), vb(128, 64, 128), vb(128, 64, 128),
            pltpu.VMEM((64, 128), jnp.int32), pltpu.VMEM((64, 128), jnp.int32), vm(128, 128), vm(128, 128),
            vm(4, 64, 32), vm(2, 1024, 128), vb(2, 2, 16, 64, 128), vb(2, 2, 16, 64, 128),
            vb(8, 16, 3, 16, 128), vm(128, 128), vb(64, 128),
            vm(128, 128), vm(64, 128), vm(128, 1024), vm(128, 512), vm(128, 128), vm(128, 128),
            vb(1792, 128), vb(16, SHARE, 128), vb(8, SHARE, 128), vb(1792, 128),
            vm(16, 8, 128), vm(8, 8, 128), vb(16, 8, 16, 128), vm(1024, 384),
            dma(2), dma(4), dma(2, 2), dma(2, 2), dma(16), dma(16), dma(8), dma(8), dma(8), dma(8),
            dma(16), dma(16), dma(16), dma(16), dma(8), dma(8), dma(8), dma(8), dma(8), dma(8),
            dma(16), dma(16), dma(16), dma(16),
        ],
        compiler_params=pltpu.CompilerParams(
            collective_id=0, has_side_effects=True, vmem_limit_bytes=60 << 20
        ),
        name="pair_backward",
    )(
        pair_repr, logit_cotangent, pair_mask, single_repr, token_index.reshape(8, 128), token_index,
        pair_up, pair_gate, pair_down, head_weight, rel_table, proj_row, proj_col,
        single_gate, single_up, single_down,
    )


def solution(mesh):
    strip = P(("row", "col"), None)
    return jax.shard_map(
        local,
        mesh=mesh,
        in_specs=(P("row", "col", None), P("row", "col", None), P("row", "col"), strip) + (P(),) * 11,
        out_specs=(P("row", "col", None), strip) + (P(),) * 7
        + (P(None, ("row", "col")), P(None, ("row", "col")), strip),
        check_vma=False,
    )
```

time: 709 us -> 150 us (0.21)
  blocking collectives: 394 us -> 0 us
  Pallas kernels: 0 us -> 134 us
  waiting for transfers between devices: 106 us -> 0 us
  matrix products: 105 us -> 0 us
  other arithmetic: 34 us -> 0 us
  local copies, waits for them, and re-layouts: 37.5 us -> 13.9 us
  between operations: 15 us -> 0.69 us
  starting transfers between devices: 14.2 us -> 0 us
    all_gather x3 -> x0, blocking collectives: 228 us -> none  [the longest x1 173 us: local(): col_whole = lax.all_gather(col_piece, ('row', 'col'), axis=0, tiled=True)]
    pallas_call x0 -> x1, Pallas kernels: none -> 134 us  [local(): pl.pallas_call(kernel, out_shape=(S((128, 64, 128), B), S((8, 384), B), S...]
    dot_general x51 -> x0, matrix products: 105 us -> none  [the longest x17 50.4 us: product_left(): lax.dot_general(matrix_a, matrix_b, (((0,), (0,)), ((), ())), preferred_e...]
    psum x2 -> x0, blocking collectives: 93.5 us -> none  [the longest x1 63.7 us: local(): lax.psum((up_gate_sum, down_sum, head_sum, rel_sum, prow_sum, pcol_sum),...]
    psum x1 -> x0, waiting for transfers between devices: 92.2 us -> none  [local(): lax.psum((up_gate_sum, down_sum, head_sum, rel_sum, prow_sum, pcol_sum),...]
    unnamed x1 -> x0, blocking collectives: 49.4 us -> none
    all_to_all x1 -> x0, blocking collectives: 22.8 us -> none  [local(): lax.all_to_all(distance_part, 'col', split_axis=0, concat_axis=1, tiled=T...]
    all_to_all x2 -> x0, starting transfers between devices: 14.2 us -> none  [the longest x1 9.13 us: local(): lax.all_to_all(strips, ('row', 'col'), split_axis=1, concat_axis=0, tiled...]
  transfers between devices with their start and end apart: 3 -> 0, of which waited for: 2 -> 0; matrix products, arithmetic and copies ran while one was open for 1% -> 0% of each run, Pallas kernels for 0% -> 0%
where the time goes in v1:
time: 150 us; the launch traced here: 149 us
  Pallas kernels  134 us (89%)
  local copies, waits for them, and re-layouts  13.9 us (9%)
    pallas_call x1, Pallas kernels, local(): pl.pallas_call(kernel, out_shape=(S((128, 64, 128), B), S((8, 384), B), S...  134 us
    unnamed x29, local copies, waits for them, and re-layouts  10.6 us
    pallas_call x2, local copies, waits for them, and re-layouts, local(): pl.pallas_call(kernel, out_shape=(S((128, 64, 128), B), S((8, 384), B), S...  3.29 us

profile of v1, /device:TPU:1, one launch (start us, length us, event | category | flops | bytes accessed | tf_op | source)
XLA Modules:
  0.0 149.0 jit_solution(1132780663652762984)
XLA Ops:
  0.6 1.5 copy.27.mask
  2.1 134.4 %pair_backward.1 = (bf16[128,64,128]{2,1,0:T(8,128)(2,1)}, bf16[8,384]{1,0:T(8,128)(2,1)}, f32[128,512]{1,0:T(8,128)}, f32[128,512]{1,0:T(8,128)}, f32[512,128]{...) custom-call(bf16[128,64,128]{2,1,0:T(8,128)(2,1)} %pair_hbm.1, ...), custom_call_target="tpu_custom_call" | custom-call | tf_op jit(solution)/shard_map/pair_backward/pallas_call | solution.py:364
  136.6 1.6 %copy.28 = f32[384,12]{0,1:T(8,128)} copy(f32[384,12]{1,0:T(8,128)} %get-tuple-element.21) | data formatting | bytes 36864 | tf_op jit(solution)/shard_map/pair_backward/pallas_call | solution.py:364
  138.2 1.6 %copy.29 = f32[384,12]{0,1:T(8,128)} copy(f32[384,12]{1,0:T(8,128)} %get-tuple-element.22) | data formatting | bytes 36864 | tf_op jit(solution)/shard_map/pair_backward/pallas_call | solution.py:364
  139.9 0.0 copy-start.8
  139.9 0.0 copy-start.2
  139.9 0.0 copy-start.1
  139.9 0.0 copy-start
  139.9 0.0 copy-start.5
  139.9 0.0 copy-start.6
  139.9 0.0 copy-start.4
  139.9 3.2 %copy.40 = bf16[128,64,128]{2,1,0:T(8,128)(2,1)} copy(bf16[128,64,128]{2,1,0:T(8,128)(2,1)} %get-tuple-element.36) | data formatting | bytes 4194304
  143.1 0.0 copy-done.8
  143.1 0.0 copy-start.3
  143.1 0.0 copy-start.7
  143.1 0.6 copy.41
  143.7 0.0 copy-done.2
  143.7 0.7 copy.42
  144.4 0.0 copy-done.1
  144.4 0.7 copy.43
  145.1 0.0 copy-done
  145.1 0.7 copy.44
  145.8 0.0 copy-done.5
  145.8 0.6 copy.45
  146.4 0.0 copy-done.6
  146.4 0.6 copy.46
  147.0 0.0 copy-done.4
  147.0 0.7 copy.47
  147.7 0.0 copy-done.3
  147.7 0.7 copy.48
  148.4 0.0 copy-done.7
  148.4 0.6 copy.49
Async XLA Ops:
  139.9 3.2 %copy-start.8 = (bf16[8,384]{1,0:T(8,128)(2,1)S(1)}, bf16[8,384]{1,0:T(8,128)(2,1)}, u32[]{:S(2)}) copy-start(bf16[8,384]{1,0:T(8,128)(2,1)} %get-tuple-element.37) | copy-start | bytes 18436
  139.9 3.8 %copy-start.2 = (f32[128,512]{1,0:T(8,128)S(1)}, f32[128,512]{1,0:T(8,128)}, u32[]{:S(2)}) copy-start(f32[128,512]{1,0:T(8,128)} %get-tuple-element.38) | copy-start | bytes 786436
  139.9 4.5 %copy-start.1 = (f32[128,512]{1,0:T(8,128)S(1)}, f32[128,512]{1,0:T(8,128)}, u32[]{:S(2)}) copy-start(f32[128,512]{1,0:T(8,128)} %get-tuple-element.39) | copy-start | bytes 786436
  139.9 5.2 %copy-start = (f32[512,128]{1,0:T(8,128)S(1)}, f32[512,128]{1,0:T(8,128)}, u32[]{:S(2)}) copy-start(f32[512,128]{1,0:T(8,128)} %get-tuple-element.40) | copy-start | bytes 786436
  139.9 5.9 %copy-start.5 = (f32[128,128]{1,0:T(8,128)S(1)}, f32[128,128]{1,0:T(8,128)}, u32[]{:S(2)}) copy-start(f32[128,128]{1,0:T(8,128)} %get-tuple-element.41) | copy-start | bytes 196612
  139.9 6.5 %copy-start.6 = (f32[65,128]{1,0:T(8,128)S(1)}, f32[65,128]{1,0:T(8,128)}, u32[]{:S(2)}) copy-start(f32[65,128]{1,0:T(8,128)} %get-tuple-element.42) | copy-start | bytes 99844
  139.9 7.1 %copy-start.4 = (f32[384,128]{1,0:T(8,128)S(1)}, f32[384,128]{1,0:T(8,128)}, u32[]{:S(2)}) copy-start(f32[384,128]{1,0:T(8,128)} %get-tuple-element.43) | copy-start | bytes 589828
  143.1 4.6 %copy-start.3 = (f32[384,128]{1,0:T(8,128)S(1)}, f32[384,128]{1,0:T(8,128)}, u32[]{:S(2)}) copy-start(f32[384,128]{1,0:T(8,128)} %get-tuple-element.44) | copy-start | bytes 589828
  143.1 5.3 %copy-start.7 = (f32[12,384]{1,0:T(8,128)S(1)}, f32[12,384]{1,0:T(8,128)}, u32[]{:S(2)}) copy-start(f32[12,384]{1,0:T(8,128)} %get-tuple-element.47) | copy-start | bytes 55300

commit v2 on v1

--- a/solution.py
+++ b/solution.py
@@ -36,11 +36,12 @@
 
 def kernel(
     pair_hbm, cot_hbm, mask, single, tok, tok_s, up, gate, down, head, rel, prow, pcol,
-    sgate, sup, sdown,
+    sgate_hbm, sup_hbm, sdown_hbm,
     og, osg, oup, ogate, odown, ohead, orel, opr, opc, osgate, osup, osdown,
     pairv, cotv, ogv, lo, hi, pos, srel, smask, tbuf, sendm, mirb, sb, rowp, colp,
     arow, acol, aug, adn, ahd, arl, ws, wr, w2, w3, rr, cr, tb, cots,
-    in_sem, out_sem, msend, mrecv, gsend, grecv, csend, crecv, hsend, hrecv,
+    sgate, sup, sdown, pieces, nball, uall, si12, slope12, h12, own_down,
+    in_sem, out_sem, msend, mrecv, gsend, grecv, csend, crecv, hsend, hrecv, bsend, brecv, qsend, qrecv,
     p1s, p1r, rs1, rr1, cs1, cr1, p2s, p2r, t2s, t2r, p3s, p3r, t3s, t3r,
 ):
     r = lax.axis_index("row")
@@ -51,6 +52,12 @@
     cot_in = pltpu.make_async_copy(cot_hbm, cotv, in_sem.at[0])
     cot_in.start()
     pair_in = pltpu.make_async_copy(pair_hbm, pairv, in_sem.at[1])
+    weights_in = [
+        pltpu.make_async_copy(a, b, in_sem.at[2 + k])
+        for k, (a, b) in enumerate(((sgate_hbm, sgate), (sup_hbm, sup), (sdown_hbm, sdown)))
+    ]
+    for cp in weights_in:
+        cp.start()
     pair_in.start()
 
     bar = pltpu.get_barrier_semaphore()
@@ -72,25 +79,11 @@
     hi[...] = jnp.where(lane == 64, big, jnp.where(lane > 64, -big, e))
     srel[...] = jnp.zeros_like(srel)
     srel[0:65, :] = rel[...].astype(F)
-    mt = jnp.transpose(mask[...].astype(F))
+    mt = mask[...].astype(F)
     for b in range(4):
         smask[b] = mt[:, b * 32:(b + 1) * 32]
     for a in (acol, aug, adn, ahd, arl):
         a[...] = jnp.zeros_like(a)
-
-    src = single[...].astype(F)
-    inv_rms = lax.rsqrt(jnp.mean(src * src, axis=-1, keepdims=True) + EPS)
-    normed = src * inv_rms
-    nbf = normed.astype(B)
-    s_gate = mm(nbf, sgate[...])
-    s_up = mm(nbf, sup[...])
-    s_sig = sigmoid(s_gate)
-    s_silu = s_gate * s_sig
-    s_hid = (s_silu * s_up).astype(B)
-    updated = src + mm(s_hid, sdown[...])
-    for k in range(3):
-        ks = slice(k * 128, (k + 1) * 128)
-        sb[r, c, k] = jnp.concatenate([src[:, ks], updated[:, ks]], axis=0).astype(B)
 
     pl.semaphore_wait(bar, NC + NR - jnp.where(diag, 1, 0))
 
@@ -120,6 +113,15 @@
         for cp in copies:
             cp.wait()
 
+    def sent_mirror(t):
+        for h in range(2):
+            @pl.when(jnp.logical_not(jnp.logical_and(diag, c % 2 == h)))
+            def _():
+                local_wait(sendm.at[t, h], msend.at[t, h])
+
+    src = single[...].astype(F)
+    sb[r, c, 0] = jnp.concatenate([src[:, :128], src[:, 128:256]], axis=0).astype(B)
+    sb[r, c, 1] = jnp.concatenate([src[:, 256:], src[:, 256:]], axis=0).astype(B)
     strips = col_copies(lambda j: sb.at[r, c], sb.at[r, c], gsend, grecv)
     start(strips)
 
@@ -141,7 +143,7 @@
         for t in range(2):
             for k in range(16):
                 sendm[t, h, k] = tbuf[t, pl.ds(k, 64, stride=16), :].astype(B)
-    for t in range(2):
+    def send_mirror(t):
         for h in range(2):
             own = jnp.logical_and(diag, c % 2 == h)
 
@@ -156,21 +158,47 @@
                     recv_sem=mrecv.at[c % 2, t], device_id=(c // 2, 2 * r + h), device_id_type=MESH,
                 ).start()
 
+    send_mirror(0)
+
+    for cp in weights_in:
+        cp.wait()
+    inv_rms = lax.rsqrt(jnp.mean(src * src, axis=-1, keepdims=True) + EPS)
+    normed = src * inv_rms
+    nbf = normed.astype(B)
+    s_gate = mm(nbf, sgate[...])
+    s_up = mm(nbf, sup[...])
+    s_sig = sigmoid(s_gate)
+    s_silu = s_gate * s_sig
+    s_hid = (s_silu * s_up).astype(B)
+    updated = (src + mm(s_hid, sdown[...])).astype(B)
+    row_piece = mm(updated, prow[...])
+    col_piece = mm(updated, pcol[...])
+    pieces[c] = jnp.concatenate([row_piece, col_piece], axis=0).astype(B)
+    projected = col_copies(lambda j: pieces.at[c], pieces.at[c], qsend, qrecv)
+    start(projected)
+
+    half = pl.ds(pl.multiple_of((c % 2) * 8, 8), 8)
     wait(strips)
-    row_u = [sb[r, :, k].astype(F)[:, 8:].reshape(128, 128).astype(B) for k in range(3)]
-    rowp[...] = sum(mm(row_u[k], prow[k * 128:(k + 1) * 128]) for k in range(3)).astype(B).astype(F)
-
+    spread = row_copies(lambda j: sb.at[r, half], sb.at[r, half], hsend, hrecv)
+    start(spread)
+
+    wait(projected)
+    both = pieces[...].astype(F)
+    rowp[...] = both[:, :8].reshape(128, 128)
     cols = row_copies(lambda j: colp, colp, csend, crecv)
 
     @pl.when(diag)
     def _():
-        full = sum(mm(row_u[k], pcol[k * 128:(k + 1) * 128]) for k in range(3))
-        pos[...] = full
+        pos[...] = both[:, 8:].reshape(128, 128)
         colp[...] = pos[pl.ds((c % 2) * 64, 64), :].astype(B)
         start(cols)
 
-    spread = row_copies(lambda j: sb.at[r], sb.at[r], hsend, hrecv)
-    start(spread)
+    def to_sibling(d):
+        rows = sb.at[lax.rem(r + NR - d, NR), half]
+        return pltpu.make_async_remote_copy(
+            src_ref=rows, dst_ref=rows, send_sem=bsend.at[d], recv_sem=brecv.at[d],
+            device_id=(r, c + 1 - 2 * (c % 2)), device_id_type=MESH,
+        )
 
     @pl.when(jnp.logical_not(diag))
     def _():
@@ -183,6 +211,44 @@
     def _():
         for cp in cols:
             cp.wait_send()
+
+    wait(spread)
+    for d in range(1, NR):
+        to_sibling(d).start()
+    sent_mirror(0)
+    send_mirror(1)
+
+    def every_token():
+        picks = lax.broadcasted_iota(jnp.int32, (128, 1536), 1)
+        unit = lax.broadcasted_iota(jnp.int32, (128, 1536), 0)
+        pick = jnp.where((picks == joint * 12 + unit) & (unit < 12), F(1), F(0)).astype(B)
+        own_gate = nt(pick, sgate[...]).astype(B)
+        own_up = nt(pick, sup[...]).astype(B)
+        own_down[...] = mm(pick, sdown[...]).astype(B)
+
+        @pl.loop(0, 4)
+        def _(q):
+            rows = pl.ds(pl.multiple_of(q * 256, 256), 256)
+            v = sb[pl.ds(q * 2, 2)].astype(F)
+            s_all = jnp.concatenate(
+                [
+                    v[:, :, 0, :8].reshape(256, 128), v[:, :, 0, 8:].reshape(256, 128),
+                    v[:, :, 1, :8].reshape(256, 128),
+                ],
+                axis=1,
+            )
+            nb = (s_all * lax.rsqrt(jnp.mean(s_all * s_all, axis=-1, keepdims=True) + EPS)).astype(B)
+            nball[rows] = nb
+            gate_all = mm(nb, sgate[...])
+            hid_all = (gate_all * sigmoid(gate_all) * mm(nb, sup[...])).astype(B)
+            uall[rows] = (s_all + mm(hid_all, sdown[...])).astype(B)
+            g12 = nt(nb, own_gate)
+            u12 = nt(nb, own_up)
+            sg12 = sigmoid(g12)
+            silu = g12 * sg12
+            si12[rows] = silu
+            slope12[rows] = u12 * (sg12 + silu * (1.0 - sg12))
+            h12[rows] = (silu * u12).astype(B)
 
     pair_in.wait()
     lane3 = lax.broadcasted_iota(jnp.int32, (1, 1, 128), 2)
@@ -240,6 +306,12 @@
         ahd[...] += tn(po, hc)
         arl[...] += tn(hot, gxb)
 
+        @pl.when(b == 1)
+        def _():
+            for d in range(1, NR):
+                to_sibling(d).wait()
+            every_token()
+
     for k in range(8):
         ws[k * 128:(k + 1) * 128] = aug[:, k * 128:(k + 1) * 128].astype(B)
     for k in range(4):
@@ -257,26 +329,6 @@
     wr[c] = ws[share(c)]
     rr[c] = arow[strip(c)]
     cr[r] = acol[strip(r)]
-
-    wait(spread)
-    s_all = [sb[:, :, k].astype(F)[:, :, :8].reshape(1024, 128) for k in range(3)]
-    u_all = jnp.concatenate(
-        [sb[:, :, k].astype(F)[:, :, 8:].reshape(1024, 128).astype(B) for k in range(3)], axis=1
-    )
-    s_all = jnp.concatenate(s_all, axis=1)
-    nb_all = (s_all * lax.rsqrt(jnp.mean(s_all * s_all, axis=-1, keepdims=True) + EPS)).astype(B)
-    picks = lax.broadcasted_iota(jnp.int32, (128, 1536), 1)
-    unit = lax.broadcasted_iota(jnp.int32, (128, 1536), 0)
-    pick = jnp.where((picks == joint * 12 + unit) & (unit < 12), F(1), F(0)).astype(B)
-    own_gate = nt(pick, sgate[...]).astype(B)
-    own_up = nt(pick, sup[...]).astype(B)
-    own_down = mm(pick, sdown[...]).astype(B)
-    g12 = nt(nb_all, own_gate)
-    u12 = nt(nb_all, own_up)
-    sg12 = sigmoid(g12)
-    si12 = g12 * sg12
-    slope12 = u12 * (sg12 + si12 * (1.0 - sg12))
-    h12 = (si12 * u12).astype(B)
 
     wait(s_row)
     wait(s_col)
@@ -315,14 +367,14 @@
     cot_all = nt(row_all, prow[...]) + nt(col_all, pcol[...])
     cots[...] = cot_all
     cb = cot_all.astype(B)
-    gsh = nt(cb, own_down)
-    gsu = (gsh * si12).astype(B)
-    gsg = (gsh * slope12).astype(B)
-    osgate[...] = tn(nb_all, gsg)[:, :12] * scale
-    osup[...] = tn(nb_all, gsu)[:, :12] * scale
-    osdown[...] = tn(h12, cb)[:12] * scale
-    opr[...] = tn(u_all, row_all) * scale
-    opc[...] = tn(u_all, col_all) * scale
+    gsh = nt(cb, own_down[...])
+    gsu = (gsh * si12[...]).astype(B)
+    gsg = (gsh * slope12[...]).astype(B)
+    osgate[...] = tn(gsg, nball[...])[:12] * scale
+    osup[...] = tn(gsu, nball[...])[:12] * scale
+    osdown[...] = tn(h12[...], cb)[:12] * scale
+    opr[...] = tn(uall[...], row_all) * scale
+    opc[...] = tn(uall[...], col_all) * scale
     c8 = cots[pl.ds(pl.multiple_of(joint * 8, 8), 8), :]
     g8 = nt(c8.astype(B), sdown[...])
     gu8 = (g8 * s_silu).astype(B)
@@ -341,14 +393,35 @@
     ohead[...] = w3[1536:1664].astype(F) * scale
     orel[...] = (w3[1664:1792].astype(F) * scale)[:65]
 
-    for t in range(2):
-        for h in range(2):
-            @pl.when(jnp.logical_not(jnp.logical_and(diag, c % 2 == h)))
-            def _():
-                local_wait(sendm.at[t, h], msend.at[t, h])
+    sent_mirror(1)
     for b in range(4):
         i0 = (b % 2) * 64 + (b // 2) * 32
         pltpu.make_async_copy(ogv.at[pl.ds(i0, BR)], og.at[pl.ds(i0, BR)], out_sem.at[b]).wait()
+
+
+def hand_over(*refs):
+    ins, outs, held, sem_in, sem_out = refs[:12], refs[12:24], refs[24:36], refs[36], refs[37]
+    parts = []
+    for k in range(12):
+        if k == 0:
+            parts += [(k, pl.ds(p * 32, 32)) for p in range(4)]
+        else:
+            parts += [(k, slice(None))]
+    into = [
+        pltpu.make_async_copy(ins[k].at[rows], held[k].at[rows], sem_in.at[n])
+        for n, (k, rows) in enumerate(parts)
+    ]
+    out = [
+        pltpu.make_async_copy(held[k].at[rows], outs[k].at[rows], sem_out.at[n])
+        for n, (k, rows) in enumerate(parts)
+    ]
+    for cp in into:
+        cp.start()
+    for a, b in zip(into, out):
+        a.wait()
+        b.start()
+    for cp in out:
+        cp.wait()
 
 
 def local(
@@ -361,24 +434,27 @@
     vm = lambda *shape: pltpu.VMEM(shape, F)
     vb = lambda *shape: pltpu.VMEM(shape, B)
     dma = lambda *shape: pltpu.SemaphoreType.DMA(shape)
-    return pl.pallas_call(
+    outs = pl.pallas_call(
         kernel,
         out_shape=(
             S((128, 64, 128), B), S((8, 384), B), S((128, 512)), S((128, 512)), S((512, 128)),
-            S((128, 128)), S((65, 128)), S((384, 128)), S((384, 128)), S((384, 12)), S((384, 12)),
+            S((128, 128)), S((65, 128)), S((384, 128)), S((384, 128)), S((12, 384)), S((12, 384)),
             S((12, 384)),
         ),
-        in_specs=[H, H, V, V, V, pl.BlockSpec(memory_space=pltpu.SMEM)] + [V] * 10,
+        in_specs=[H, H, V, V, V, pl.BlockSpec(memory_space=pltpu.SMEM)] + [V] * 7 + [H] * 3,
         out_specs=[H] + [V] * 11,
         scratch_shapes=[
             vb(128, 64, 128), vb(128, 64, 128), vb(128, 64, 128),
             pltpu.VMEM((64, 128), jnp.int32), pltpu.VMEM((64, 128), jnp.int32), vm(128, 128), vm(128, 128),
             vm(4, 64, 32), vm(2, 1024, 128), vb(2, 2, 16, 64, 128), vb(2, 2, 16, 64, 128),
-            vb(8, 16, 3, 16, 128), vm(128, 128), vb(64, 128),
+            vb(8, 16, 2, 16, 128), vm(128, 128), vb(64, 128),
             vm(128, 128), vm(64, 128), vm(128, 1024), vm(128, 512), vm(128, 128), vm(128, 128),
             vb(1792, 128), vb(16, SHARE, 128), vb(8, SHARE, 128), vb(1792, 128),
             vm(16, 8, 128), vm(8, 8, 128), vb(16, 8, 16, 128), vm(1024, 384),
-            dma(2), dma(4), dma(2, 2), dma(2, 2), dma(16), dma(16), dma(8), dma(8), dma(8), dma(8),
+            vb(384, 1536), vb(384, 1536), vb(1536, 384), vb(16, 16, 128), vb(1024, 384), vb(1024, 384),
+            vm(1024, 128), vm(1024, 128), vb(1024, 128), vb(128, 384),
+            dma(5), dma(4), dma(2, 2), dma(2, 2), dma(16), dma(16), dma(8), dma(8), dma(8), dma(8), dma(8),
+            dma(8), dma(16), dma(16),
             dma(16), dma(16), dma(16), dma(16), dma(8), dma(8), dma(8), dma(8), dma(8), dma(8),
             dma(16), dma(16), dma(16), dma(16),
         ],
@@ -387,10 +463,19 @@
         ),
         name="pair_backward",
     )(
-        pair_repr, logit_cotangent, pair_mask, single_repr, token_index.reshape(8, 128), token_index,
+        pair_repr, logit_cotangent, pair_mask.T, single_repr, token_index.reshape(8, 128), token_index,
         pair_up, pair_gate, pair_down, head_weight, rel_table, proj_row, proj_col,
         single_gate, single_up, single_down,
     )
+    outs = pl.pallas_call(
+        hand_over,
+        out_shape=[S(o.shape, o.dtype) for o in outs],
+        in_specs=[H] * 12,
+        out_specs=[H] * 12,
+        scratch_shapes=[pltpu.VMEM(o.shape, o.dtype) for o in outs] + [dma(15), dma(15)],
+        name="hand_over",
+    )(*outs)
+    return (*outs[:9], outs[9].T, outs[10].T, outs[11])
 
 
 def solution(mesh):

time: 150 us -> 120 us (0.80)
  Pallas kernels: 134 us -> 119 us
  local copies, waits for them, and re-layouts: 13.9 us -> 0 us
    pallas_call x1, Pallas kernels: 134 us -> 116 us  [local(): pl.pallas_call(kernel, out_shape=(S((128, 64, 128), B), S((8, 384), B), S...]
    unnamed x29 -> x0, local copies, waits for them, and re-layouts: 10.6 us -> none
    pallas_call x2 -> x0, local copies, waits for them, and re-layouts: 3.29 us -> none  [local(): pl.pallas_call(kernel, out_shape=(S((128, 64, 128), B), S((8, 384), B), S...]
    pallas_call x0 -> x1, Pallas kernels: none -> 3.06 us  [local(): pl.pallas_call(hand_over, out_shape=[S(o.shape, o.dtype) for o in outs],...]
where the time goes in v2:
time: 120 us
  Pallas kernels  119 us (99%)
    pallas_call x1, Pallas kernels, local(): pl.pallas_call(kernel, out_shape=(S((128, 64, 128), B), S((8, 384), B), S...  116 us
    pallas_call x1, Pallas kernels, local(): pl.pallas_call(hand_over, out_shape=[S(o.shape, o.dtype) for o in outs],...  3.06 us

profile of v2, /device:TPU:1, one launch (start us, length us, event | category | flops | bytes accessed | tf_op | source)
XLA Modules:
  0.0 120.0 jit_solution(14106011429720996827)
XLA Ops:
  0.7 116.1 %pair_backward.1 = (bf16[128,64,128]{2,1,0:T(8,128)(2,1)}, bf16[8,384]{1,0:T(8,128)(2,1)}, f32[128,512]{1,0:T(8,128)}, f32[128,512]{1,0:T(8,128)}, f32[512,128]{...) custom-call(bf16[128,64,128]{2,1,0:T(8,128)(2,1)} %pair_hbm.1, ...), custom_call_target="tpu_custom_call" | custom-call | tf_op jit(solution)/shard_map/pair_backward/pallas_call | solution.py:437
  116.8 3.1 %hand_over.1 = (bf16[128,64,128]{2,1,0:T(8,128)(2,1)}, bf16[8,384]{1,0:T(8,128)(2,1)}, f32[128,512]{1,0:T(8,128)}, f32[128,512]{1,0:T(8,128)}, f32[512,128]{1,0:...) custom-call(bf16[128,64,128]{2,1,0:T(8,128)(2,1)} %get-tuple-element, ...), custom_call_target="tpu_custom_call" | custom-call | tf_op jit(solution)/shard_map/hand_over/pallas_call | solution.py:470

commit v3 on v2

--- a/solution.py
+++ b/solution.py
@@ -124,6 +124,23 @@
     sb[r, c, 1] = jnp.concatenate([src[:, 256:], src[:, 256:]], axis=0).astype(B)
     strips = col_copies(lambda j: sb.at[r, c], sb.at[r, c], gsend, grecv)
     start(strips)
+
+    def send_mirror(t, h):
+        own = jnp.logical_and(diag, c % 2 == h)
+
+        @pl.when(own)
+        def _():
+            pltpu.make_async_copy(sendm.at[t, h], mirb.at[c % 2, t], mrecv.at[c % 2, t]).start()
+
+        @pl.when(jnp.logical_not(own))
+        def _():
+            pltpu.make_async_remote_copy(
+                src_ref=sendm.at[t, h], dst_ref=mirb.at[c % 2, t], send_sem=msend.at[t, h],
+                recv_sem=mrecv.at[c % 2, t], device_id=(c // 2, 2 * r + h), device_id_type=MESH,
+            ).start()
+
+    half = pl.ds(pl.multiple_of((c % 2) * 8, 8), 8)
+    spread = row_copies(lambda j: sb.at[r, half], sb.at[r, half], hsend, hrecv)
 
     cot_in.wait()
     half_lane = lax.broadcasted_iota(jnp.int32, (16, 128), 1) < 64
@@ -143,23 +160,10 @@
         for t in range(2):
             for k in range(16):
                 sendm[t, h, k] = tbuf[t, pl.ds(k, 64, stride=16), :].astype(B)
-    def send_mirror(t):
-        for h in range(2):
-            own = jnp.logical_and(diag, c % 2 == h)
-
-            @pl.when(own)
-            def _():
-                pltpu.make_async_copy(sendm.at[t, h], mirb.at[c % 2, t], mrecv.at[c % 2, t]).start()
-
-            @pl.when(jnp.logical_not(own))
-            def _():
-                pltpu.make_async_remote_copy(
-                    src_ref=sendm.at[t, h], dst_ref=mirb.at[c % 2, t], send_sem=msend.at[t, h],
-                    recv_sem=mrecv.at[c % 2, t], device_id=(c // 2, 2 * r + h), device_id_type=MESH,
-                ).start()
-
-    send_mirror(0)
-
+        if h == 0:
+            wait(strips)
+            start(spread)
+        send_mirror(0, h)
     for cp in weights_in:
         cp.wait()
     inv_rms = lax.rsqrt(jnp.mean(src * src, axis=-1, keepdims=True) + EPS)
@@ -177,11 +181,6 @@
     projected = col_copies(lambda j: pieces.at[c], pieces.at[c], qsend, qrecv)
     start(projected)
 
-    half = pl.ds(pl.multiple_of((c % 2) * 8, 8), 8)
-    wait(strips)
-    spread = row_copies(lambda j: sb.at[r, half], sb.at[r, half], hsend, hrecv)
-    start(spread)
-
     wait(projected)
     both = pieces[...].astype(F)
     rowp[...] = both[:, :8].reshape(128, 128)
@@ -216,7 +215,8 @@
     for d in range(1, NR):
         to_sibling(d).start()
     sent_mirror(0)
-    send_mirror(1)
+    send_mirror(1, 0)
+    send_mirror(1, 1)
 
     def every_token():
         picks = lax.broadcasted_iota(jnp.int32, (128, 1536), 1)

time: 120 us -> 116 us (0.967)
  Pallas kernels: 119 us -> 115 us
    pallas_call x1, Pallas kernels: 116 us -> 112 us  [local(): pl.pallas_call(kernel, out_shape=(S((128, 64, 128), B), S((8, 384), B), S...]
where the time goes in v3:
time: 116 us
  Pallas kernels  115 us (99%)
    pallas_call x1, Pallas kernels, local(): pl.pallas_call(kernel, out_shape=(S((128, 64, 128), B), S((8, 384), B), S...  112 us
    pallas_call x1, Pallas kernels, local(): pl.pallas_call(hand_over, out_shape=[S(o.shape, o.dtype) for o in outs],...  3.06 us

profile of v3, /device:TPU:1, one launch (start us, length us, event | category | flops | bytes accessed | tf_op | source)
XLA Modules:
  0.0 115.9 jit_solution(12306495689842828752)
XLA Ops:
  0.7 112.1 %pair_backward.1 = (bf16[128,64,128]{2,1,0:T(8,128)(2,1)}, bf16[8,384]{1,0:T(8,128)(2,1)}, f32[128,512]{1,0:T(8,128)}, f32[128,512]{1,0:T(8,128)}, f32[512,128]{...) custom-call(bf16[128,64,128]{2,1,0:T(8,128)(2,1)} %pair_hbm.1, ...), custom_call_target="tpu_custom_call" | custom-call | tf_op jit(solution)/shard_map/pair_backward/pallas_call | solution.py:437
  112.7 3.1 %hand_over.1 = (bf16[128,64,128]{2,1,0:T(8,128)(2,1)}, bf16[8,384]{1,0:T(8,128)(2,1)}, f32[128,512]{1,0:T(8,128)}, f32[128,512]{1,0:T(8,128)}, f32[512,128]{1,0:...) custom-call(bf16[128,64,128]{2,1,0:T(8,128)(2,1)} %get-tuple-element, ...), custom_call_target="tpu_custom_call" | custom-call | tf_op jit(solution)/shard_map/hand_over/pallas_call | solution.py:470
